TPU v7x, 32 devices: a whole 2x2x4 slice. The times are simulated.
32 devices in a mesh: dom: 2 (over x), space: 16 (over z, y, core).
Axes of the slice: x: 2, y: 2, z: 4, core: 2. Of those that a mesh axis runs over, the one named last changes fastest.
Arguments:
- inputs: bfloat16 [2, 32, 2048, 2048], P('dom', None, 'space'), parts along dimension 0, may hold values from -10.5 to 10.5
- target: bfloat16 [2, 32, 2048, 2048], P('dom', None, 'space'), parts along dimension 0, may hold values from -6 to 6
- spectral_weight: float32 [64, 32, 32, 128], P('space'), may hold values from -18 to 18
- local_weight: bfloat16 [32, 32], replicated, may hold values from -1 to 1
- bias_term: float32 [32], replicated, may hold values from -3 to 3
Outputs:
- grad_input: bfloat16 [2, 32, 2048, 2048], P('dom', None, 'space'), parts along dimension 0
- grad_spectral: float32 [64, 64, 32, 128], P('space', 'dom'), parts along dimension 1
- grad_local: float32 [64, 32], P('dom'), parts along dimension 0
- grad_bias: float32 [64], P('dom'), parts along dimension 0
There are 2 independent parts, one for each index of `dom`. A program takes and returns all parts, laid end to end along the dimension named above; an argument that names none is the same for every part. Nothing has to cross between parts.
All inputs are finite; a program needn't handle non-finite values.
Results may differ from a plain program's by a relative error of at most 0.014.
Values may be sent and summed in bfloat16 or wider, within the bound.
A program may use at most 192 MiB of HBM per device.

v0:
```python
import math
import jax
import jax.numpy as jnp
from jax import lax
from jax.sharding import PartitionSpec as P

H = 2048
W = 2048
KX = 64
KY = 64
PRECISE = lax.Precision.HIGHEST


def row_table():
    mode_index = jnp.arange(KY, dtype=jnp.int32)[:, None]
    column = jnp.arange(W, dtype=jnp.int32)[None, :]
    angles = (mode_index * column % W).astype(jnp.float32) * (2.0 * math.pi / W)
    factor = 1.0 / math.sqrt(H * W)
    return jnp.stack([jnp.cos(angles) * factor, -jnp.sin(angles) * factor]).astype(jnp.bfloat16)


def column_table(row_index):
    column = jnp.arange(KX, dtype=jnp.int32)
    frequency = jnp.where(column < KX // 2, column, column + H - KX)
    angles = (row_index[:, None] * frequency[None, :] % H).astype(jnp.float32) * (2.0 * math.pi / H)
    return jnp.concatenate([jnp.cos(angles), jnp.sin(angles)], axis=1)


def mode_weights(start_mode, mode_count):
    mode_index = start_mode + jnp.arange(mode_count, dtype=jnp.int32)
    return jnp.where(mode_index == 0, 1.0, 2.0).astype(jnp.float32)


def row_analysis(field_data, basis):
    return jnp.einsum("schw,pkw->kpsch", field_data, basis, preferred_element_type=jnp.float32)


def row_synth(spectra, basis):
    return jnp.einsum("kpsch,pkw->schw", spectra, basis, preferred_element_type=jnp.float32)


def column_modes(slab_part, basis):
    product = jnp.einsum("kpsch,hj->kpscj", slab_part, basis, precision=PRECISE)
    half_count = basis.shape[1] // 2
    real_part = product[:, 0, :, :, :half_count] + product[:, 1, :, :, half_count:]
    imag_part = product[:, 1, :, :, :half_count] - product[:, 0, :, :, half_count:]
    return jnp.concatenate([real_part, imag_part], axis=-1)


def column_synth(mode_data, basis):
    half_count = basis.shape[1] // 2
    real_part, imag_part = (mode_data[..., :half_count], mode_data[..., half_count:])
    cosines, sine_part = (basis[:, :half_count], basis[:, half_count:])
    first_part = jnp.einsum("ysok,hk->ysoh", real_part, cosines, precision=PRECISE) - jnp.einsum(
        "ysok,hk->ysoh", imag_part, sine_part, precision=PRECISE
    )
    second = jnp.einsum("ysok,hk->ysoh", real_part, sine_part, precision=PRECISE) + jnp.einsum(
        "ysok,hk->ysoh", imag_part, cosines, precision=PRECISE
    )
    return jnp.stack([first_part, second], axis=1).astype(jnp.bfloat16)


def split_complex(mode_data):
    half_count = mode_data.shape[-1] // 2
    return (mode_data[..., :half_count], mode_data[..., half_count:])


def mix_modes(input_modes, weight):
    spec_real, spec_imag = split_complex(input_modes)
    weight_real, weight_imag = split_complex(weight)
    form = "ysck,ycok->ysok"
    out_real = jnp.einsum(form, spec_real, weight_real, precision=PRECISE) - jnp.einsum(
        form, spec_imag, weight_imag, precision=PRECISE
    )
    out_imag = jnp.einsum(form, spec_real, weight_imag, precision=PRECISE) + jnp.einsum(
        form, spec_imag, weight_real, precision=PRECISE
    )
    return jnp.concatenate([out_real, out_imag], axis=-1)


def mix_back(delta_modes, weight):
    delta_real, delta_imag = split_complex(delta_modes)
    weight_real, weight_imag = split_complex(weight)
    form = "ysok,ycok->ysck"
    out_real = jnp.einsum(form, delta_real, weight_real, precision=PRECISE) + jnp.einsum(
        form, delta_imag, weight_imag, precision=PRECISE
    )
    out_imag = jnp.einsum(form, delta_imag, weight_real, precision=PRECISE) - jnp.einsum(
        form, delta_real, weight_imag, precision=PRECISE
    )
    return jnp.concatenate([out_real, out_imag], axis=-1)


def mix_grad(input_modes, delta_modes):
    spec_real, spec_imag = split_complex(input_modes)
    delta_real, delta_imag = split_complex(delta_modes)
    form = "ysck,ysok->ycok"
    grad_real = jnp.einsum(form, spec_real, delta_real, precision=PRECISE) + jnp.einsum(
        form, spec_imag, delta_imag, precision=PRECISE
    )
    grad_imag = jnp.einsum(form, spec_real, delta_imag, precision=PRECISE) - jnp.einsum(
        form, spec_imag, delta_real, precision=PRECISE
    )
    return jnp.concatenate([grad_real, grad_imag], axis=-1)


def gelu_parts(value):
    normal_cdf = 0.5 * (1.0 + jax.scipy.special.erf(value * (1.0 / math.sqrt(2.0))))
    density = jnp.exp(-0.5 * value * value) * (1.0 / math.sqrt(2.0 * math.pi))
    return (value * normal_cdf, normal_cdf + value * density)


def per_device(inputs, target, spectral_weight, local_weight, bias_term):
    mode_block = spectral_weight.shape[0]
    row_count = inputs.shape[2]
    device = lax.axis_index("space")
    row_basis = row_table()
    column_basis = column_table(jnp.arange(H, dtype=jnp.int32))
    own_basis = column_table(device * row_count + jnp.arange(row_count, dtype=jnp.int32))
    mode_gain = mode_weights(device * mode_block, mode_block)[:, None, None, None]

    def to_modes(field_data):
        row_modes = row_analysis(field_data, row_basis)
        return lax.psum_scatter(
            column_modes(row_modes, own_basis), "space", scatter_dimension=0, tiled=True
        )

    def to_rows(mode_data):
        column_part = column_synth(mode_data, column_basis)
        return row_synth(
            lax.all_to_all(column_part, "space", split_axis=4, concat_axis=0, tiled=True), row_basis
        )

    input_modes = to_modes(inputs)
    mixed_modes = mix_modes(input_modes, spectral_weight) * mode_gain
    local_term = jnp.einsum(
        "co,schw->sohw", local_weight, inputs, preferred_element_type=jnp.float32
    )
    preact = to_rows(mixed_modes) + local_term + bias_term[None, :, None, None]
    activated, derivative = gelu_parts(preact)
    delta_pre = ((activated - target.astype(jnp.float32)) * derivative).astype(jnp.bfloat16)
    delta_modes = to_modes(delta_pre) * mode_gain
    grad_spectral = mix_grad(input_modes, delta_modes)
    back_modes = mix_back(delta_modes, spectral_weight)
    back_local = jnp.einsum(
        "co,sohw->schw", local_weight, delta_pre, preferred_element_type=jnp.float32
    )
    grad_input = (to_rows(back_modes) + back_local).astype(jnp.bfloat16)
    weight_term = jnp.einsum("schw,sohw->co", inputs, delta_pre, preferred_element_type=jnp.float32)
    bias_sum = jnp.sum(delta_pre, axis=(0, 2, 3), dtype=jnp.float32)
    weight_total, bias_total = lax.psum((weight_term, bias_sum), "space")
    cell_count = inputs.shape[0] * H * W
    return (grad_input, grad_spectral, weight_total / cell_count, bias_total / cell_count)


def solution(mesh):
    return jax.shard_map(
        per_device,
        mesh=mesh,
        in_specs=(
            P("dom", None, "space", None),
            P("dom", None, "space", None),
            P("space", None, None, None),
            P(),
            P(),
        ),
        out_specs=(
            P("dom", None, "space", None),
            P("space", "dom", None, None),
            P("dom", None),
            P("dom"),
        ),
        check_vma=False,
    )
```

profile of v0, /device:TPU:0, one launch (start us, length us, event | category | flops | bytes accessed | tf_op | source)
XLA Modules:
  0.0 490.5 jit_solution(4571138129678116677)
XLA Ops:
  7.2 0.0 copy-start
  7.2 0.0 reduce-scatter.3.cloned.1.call-start
  7.2 2.2 multiply_convert_fusion
  9.4 0.3 fusion.101
  9.8 0.0 copy-start.1
  9.8 10.8 %fusion.37 = f32[64,2,32,128]{3,0,2,1:T(8,128)} fusion(bf16[1,32,128,2048]{3,2,1,0:T(8,128)(2,1)} %param.5, bf16[1,64,2048]{2,1,0:T(8,128)(2,1)S(1)} %get-tuple-element.42, bf16[1,64,2048]{2,1,0:T(8,128)(2,1)S(1)} %get-tuple-element.43), kind=kOutput, calls=%fused_computation.52 | convolution fusion | flops 2148532224 | bytes 19398656 | tf_op jit(solution)/shard_map/schw,pkw->kpsch/dot_general | solution.py:35
  20.6 4.9 fusion.31
  25.5 0.3 fusion.50
  25.8 0.3 fusion.52
  26.2 1.3 pad_maximum_fusion.1
  27.5 0.0 reduce-scatter.3.cloned.1.call-update
  27.5 60.3 %reduce-scatter.3.cloned.1.call-done = f32[4,1,32,128]{3,2,0,1:T(8,128)} async-done(((f32[64,1,32,128]{3,2,0,1:T(8,128)}), f32[4,1,32,128]{3,2,0,1:T(8,128)}) %reduce-scatter.3.cloned.1.call-update) | async-done | bytes 65552 | tf_op jit(solution)/shard_map/reduce_scatter | solution.py:124
  87.8 1.0 slice_bitcast_fusion.7
  88.8 0.0 copy-done.1
  88.8 1.0 multiply_reduce_fusion.6
  89.9 0.1 maximum_multiply_fusion
  90.0 2.9 fusion.62
  92.9 2.9 fusion.69
  95.8 3.6 fusion.25
  99.4 3.2 fusion.26
  102.7 1.1 pad_maximum_fusion.2
  103.7 6.8 %copy.27 = bf16[4,2,1,32,2048]{3,0,2,1,4:T(4,128)(2,1)} copy(bf16[4,2,1,32,2048]{4,3,0,2,1:T(8,128)(2,1)} %pad_maximum_fusion.2) | data formatting | bytes 2097152 | tf_op jit(solution)/shard_map/stack | solution.py:60
  110.5 7.7 %reshape.437 = bf16[16,2,16384]{2,1,0:T(2,128)(2,1)} reshape(bf16[2048,2,1,4,32]{4,3,2,1,0:T(4,128)(2,1)} %bitcast.233) | data formatting | bytes 2097152
  118.2 4.3 all-to-all-start
  122.5 0.0 reduce-scatter.5.cloned.1.call-start
  122.6 0.0 copy-done
  122.6 0.0 copy-start.3
  122.6 22.5 %fusion.17 = f32[128,2048,32]{1,2,0:T(8,128)} fusion(bf16[32,128,2048]{2,1,0:T(8,128)(2,1)} %bitcast.229, bf16[32,32]{1,0:T(8,128)(2,1)S(1)} %copy-done), kind=kOutput, calls=%fused_computation.21 | convolution fusion | flops 536870912 | bytes 50333696 | tf_op jit(solution)/shard_map/co,schw->sohw/dot_general | solution.py:136
  145.1 0.3 all-to-all-done
  145.5 7.3 %reshape.438 = bf16[2048,2,1,4,32]{4,3,2,1,0:T(4,128)(2,1)} reshape(bf16[16,2,16384]{2,1,0:T(2,128)(2,1)} %all-to-all-done) | data formatting | bytes 2097152
  152.8 7.1 %copy.28 = bf16[4,2,1,32,16,128]{5,0,4,1,3,2:T(4,128)(2,1)} copy(bf16[4,2,1,32,16,128]{3,0,1,5,4,2:T(4,128)(2,1)} %bitcast.234) | data formatting | bytes 2097152 | tf_op jit(solution)/shard_map/all_to_all | solution.py:131
  159.9 0.0 copy-done.3
  159.9 38.7 %convert_reduce_fusion = (f32[32]{0:T(128)S(1)}, bf16[1,32,128,2048]{3,2,1,0:T(8,128)(2,1)}) fusion(bf16[1,32,128,2048]{3,2,1,0:T(8,128)(2,1)} %param.6, f32[32]{0:T(128)S(1)} %copy-done.3, f32[128,2048,32]{1,2,0:T(8,128)} %fusion.17, bf16[64,2,32,128]{3,0,1,2:T(8,128)(2,1)} %bitcast.238, bf16[1,64,2048]{2,1,0:T(8,128)(2,1)S(1)} %get-tuple-element.42, ...), kind=kOutput, calls=%fused_computation.11 | convolution fusion | flops 2290352128 | bytes 68681984 | tf_op jit(solution)/shard_map/kpsch,pkw->schw/dot_general | solution.py:39
  198.6 10.5 %fusion.40 = f32[64,2,32,128]{3,0,2,1:T(8,128)} fusion(bf16[1,32,128,2048]{3,2,1,0:T(8,128)(2,1)} %get-tuple-element.41, bf16[1,64,2048]{2,1,0:T(8,128)(2,1)S(1)} %get-tuple-element.42, bf16[1,64,2048]{2,1,0:T(8,128)(2,1)S(1)} %get-tuple-element.43), kind=kOutput, calls=%fused_computation.53 | convolution fusion | flops 2148532224 | bytes 19398656 | tf_op jit(solution)/shard_map/schw,pkw->kpsch/dot_general | solution.py:35
  209.1 4.6 fusion.34
  213.7 0.6 fusion.49
  214.3 1.3 pad_maximum_fusion.3
  215.6 0.0 reduce-scatter.5.cloned.1.call-update
  215.7 84.2 %fusion.43 = f32[32,32]{0,1:T(8,128)S(1)} fusion(bf16[32,128,2048]{2,1,0:T(8,128)(2,1)} %bitcast.230, bf16[32,128,2048]{2,1,0:T(8,128)(2,1)} %bitcast.231), kind=kOutput, calls=%fused_computation.54 | convolution fusion | flops 536870912 | bytes 33558528 | tf_op jit(solution)/shard_map/schw,sohw->co/dot_general | solution.py:149
  299.9 62.8 %all-reduce = (f32[32,32]{0,1:T(8,128)S(1)}, f32[32]{0:T(128)S(1)}) all-reduce(f32[32,32]{0,1:T(8,128)S(1)} %fusion.43, f32[32]{0:T(128)S(1)} %get-tuple-element.40), channel_id=1, replica_groups=mesh['dom'=2,'space'=16] {'space'}, use_global_device_ids=true, to_apply=%region_2.3 | all-reduce | flops 1056 | bytes 8448 | tf_op jit(solution)/shard_map/psum | solution.py:151
  362.7 0.0 reduce-scatter.5.cloned.1.call-done
  362.7 0.9 broadcast_multiply_fusion
  363.6 0.1 slice_bitcast_fusion.2
  363.7 4.3 add_bitcast_fusion
  368.0 2.9 fusion.59
  370.9 2.9 fusion.66
  373.8 3.2 fusion.23
  377.0 3.2 fusion.24
  380.3 0.1 pad_maximum_fusion.4
  380.4 5.0 %copy.34 = bf16[4,2,1,32,2048]{3,0,2,1,4:T(4,128)(2,1)} copy(bf16[4,2,1,32,2048]{4,3,0,2,1:T(8,128)(2,1)S(1)} %pad_maximum_fusion.4) | data formatting | bytes 2097152 | tf_op jit(solution)/shard_map/stack | solution.py:60
  385.4 7.6 %reshape.439 = bf16[16,2,16384]{2,1,0:T(2,128)(2,1)} reshape(bf16[2048,2,1,4,32]{4,3,2,1,0:T(4,128)(2,1)} %bitcast.235) | data formatting | bytes 2097152
  393.0 4.3 all-to-all-start.1
  397.4 0.7 copy.40
  398.0 0.5 broadcast_multiply_fusion.2
  398.6 0.0 copy-start.2
  398.6 35.7 %fusion.14 = f32[128,2048,32]{1,2,0:T(8,128)} fusion(bf16[32,128,2048]{2,1,0:T(8,128)(2,1)} %bitcast.232, bf16[32,32]{1,0:T(8,128)(2,1)S(1)} %copy-done), kind=kOutput, calls=%fused_computation.18 | convolution fusion | flops 536870912 | bytes 50333696 | tf_op jit(solution)/shard_map/co,sohw->schw/dot_general | solution.py:145
  434.2 0.0 copy-done.2
  434.2 3.6 pad_maximum_fusion
  437.8 0.0 all-to-all-done.1
  437.8 7.3 %reshape.440 = bf16[2048,2,1,4,32]{4,3,2,1,0:T(4,128)(2,1)} reshape(bf16[16,2,16384]{2,1,0:T(2,128)(2,1)} %all-to-all-done.1) | data formatting | bytes 2097152
  445.2 6.1 %copy.35 = bf16[4,2,1,32,16,128]{5,0,4,1,3,2:T(4,128)(2,1)S(1)} copy(bf16[4,2,1,32,16,128]{3,0,1,5,4,2:T(4,128)(2,1)} %bitcast.236) | data formatting | bytes 2097152 | tf_op jit(solution)/shard_map/all_to_all | solution.py:131
  451.3 31.9 %fusion.6 = bf16[1,32,128,2048]{3,2,1,0:T(8,128)(2,1)} fusion(f32[128,2048,32]{1,2,0:T(8,128)} %fusion.14, bf16[64,2,32,128]{3,0,1,2:T(8,128)(2,1)S(1)} %bitcast.237, bf16[1,64,2048]{2,1,0:T(8,128)(2,1)S(1)} %get-tuple-element.42, bf16[1,64,2048]{2,1,0:T(8,128)(2,1)S(1)} %get-tuple-element.43), kind=kOutput, calls=%fused_computation.8 | convolution fusion | flops 2164523008 | bytes 51904512 | tf_op jit(solution)/shard_map/kpsch,pkw->schw/dot_general | solution.py:39
  (6 shorter events, 0.0 us)
Async XLA Ops:
  7.2 115.4 %copy-start = (bf16[32,32]{1,0:T(8,128)(2,1)S(1)}, bf16[32,32]{1,0:T(8,128)(2,1)}, u32[]{:S(2)}) copy-start(bf16[32,32]{1,0:T(8,128)(2,1)} %param.8) | copy-start | bytes 6148
  7.2 80.6 %reduce-scatter.3.cloned.1.call-start = ((), (), s32[]{:S(2)}) async-start(), calls=%async_computation.4 | async-start | bytes 1114112 | tf_op jit(solution)/shard_map/reduce_scatter | solution.py:124
  9.8 79.0 %copy-start.1 = (f32[4,32,32,128]{3,2,1,0:T(8,128)S(1)}, f32[4,32,32,128]{3,2,1,0:T(8,128)}, u32[]{:S(2)}) copy-start(f32[4,32,32,128]{3,2,1,0:T(8,128)} %param.7) | copy-start | bytes 6291460
  118.2 27.3 %all-to-all-start = ((bf16[16,2,16384]{2,1,0:T(2,128)(2,1)}), bf16[16,2,16384]{2,1,0:T(2,128)(2,1)}, u32[]{:S(2)}, u32[]{:S(2)}) async-start(bf16[16,2,16384]{2,1,0:T(2,128)(2,1)} %reshape.437), calls=%async_computation.1 | async-start | bytes 2097152 | tf_op jit(solution)/shard_map/all_to_all | solution.py:131
  122.5 240.1 %reduce-scatter.5.cloned.1.call-start = ((), (), s32[]{:S(2)}) async-start(), calls=%async_computation.5 | async-start | bytes 1114112 | tf_op jit(solution)/shard_map/reduce_scatter | solution.py:124
  122.6 37.3 %copy-start.3 = (f32[32]{0:T(128)S(1)}, f32[32]{0:T(128)}, u32[]{:S(2)}) copy-start(f32[32]{0:T(128)} %param.9) | copy-start | bytes 388
  393.0 44.8 %all-to-all-start.1 = ((bf16[16,2,16384]{2,1,0:T(2,128)(2,1)}), bf16[16,2,16384]{2,1,0:T(2,128)(2,1)}, u32[]{:S(2)}, u32[]{:S(2)}) async-start(bf16[16,2,16384]{2,1,0:T(2,128)(2,1)} %reshape.439), calls=%async_computation.3 | async-start | bytes 2097152 | tf_op jit(solution)/shard_map/all_to_all | solution.py:131
  398.6 35.7 %copy-start.2 = (f32[4,32,32,64]{3,2,1,0:T(8,128)S(1)}, f32[4,32,32,64]{3,2,1,0:T(8,128)}, u32[]{:S(2)}) copy-start(f32[4,32,32,64]{3,2,1,0:T(8,128)} %get-tuple-element.28) | copy-start | bytes 3145732
Sparse Core Ops, SparseCore 0:
  27.6 60.1 reduce-scatter.2
  215.8 59.5 reduce-scatter.4
where the time goes:
time: 495 us; the launch traced here: 490 us
  matrix products  269 us (54%)
  blocking collectives  62.8 us (13%)
  waiting for transfers between devices  60.6 us (12%)
  local copies, waits for them, and re-layouts  56.8 us (11%)
  other arithmetic  18 us (4%)
  between operations  14.8 us (3%)
  starting transfers between devices  8.74 us (2%)
    dot_general x1, matrix products, per_device(): jnp.einsum('schw,sohw->co', inputs, delta_pre, preferred_element_type=jnp...  84.2 us
    dot_general x2, matrix products, row_synth(): jnp.einsum('kpsch,pkw->schw', spectra, basis, preferred_element_type=jnp....  70.6 us
    psum x1, blocking collectives, per_device(): weight_total, bias_total = lax.psum((weight_term, bias_sum), 'space')  62.8 us
    reduce_scatter x2, waiting for transfers between devices, to_modes(): lax.psum_scatter(column_modes(row_modes, own_basis), 'space', scatter_dim...  60.3 us
    dot_general x1, matrix products, per_device(): jnp.einsum('co,sohw->schw', local_weight, delta_pre, preferred_element_ty...  35.7 us
    unnamed x15, local copies, waits for them, and re-layouts  31.8 us
    dot_general x1, matrix products, per_device(): jnp.einsum('co,schw->sohw', local_weight, inputs, preferred_element_type=...  22.5 us
    dot_general x2, matrix products, row_analysis(): jnp.einsum('schw,pkw->kpsch', field_data, basis, preferred_element_type=j...  21.3 us
  transfers between devices with their start and end apart: 4, of which 2 were waited for; matrix products, arithmetic and copies ran while one was open for 30% of the time, Pallas kernels for 0%

commit v1 on v0

--- a/solution.py
+++ b/solution.py
@@ -9,6 +9,18 @@
 KX = 64
 KY = 64
 PRECISE = lax.Precision.HIGHEST
+
+
+def store_the_set(my_data, chip_axis):
+    return jnp.concatenate(
+        lax.all_to_all(
+            jnp.stack(jnp.split(my_data, lax.psum(1, axis_name=chip_axis), 4)),
+            axis_name=chip_axis,
+            split_axis=0,
+            concat_axis=0,
+        ),
+        0,
+    )
 
 
 def row_table():
@@ -127,9 +139,7 @@
 
     def to_rows(mode_data):
         column_part = column_synth(mode_data, column_basis)
-        return row_synth(
-            lax.all_to_all(column_part, "space", split_axis=4, concat_axis=0, tiled=True), row_basis
-        )
+        return row_synth(store_the_set(column_part, "space"), row_basis)
 
     input_modes = to_modes(inputs)
     mixed_modes = mix_modes(input_modes, spectral_weight) * mode_gain

time: 495 us -> 464 us (0.937)
  local copies, waits for them, and re-layouts: 56.8 us -> 23.7 us
    another operation x2 -> x0, local copies, waits for them, and re-layouts: 11.8 us -> none  [column_synth(): return jnp.stack([first_part, second], axis=1).astype(jnp.bfloat16)]
    unnamed x15 -> x41, local copies, waits for them, and re-layouts: 31.8 us -> 21 us
    all_to_all x2, local copies, waits for them, and re-layouts: 13.2 us -> 2.7 us  [store_the_set(): lax.all_to_all(jnp.stack(jnp.split(my_data, lax.psum(1, axis_name=chip_ax...]
    dot_general x2, matrix products: 70.6 us -> 79 us  [row_synth(): jnp.einsum('kpsch,pkw->schw', spectra, basis, preferred_element_type=jnp....]
    dot_general x1, matrix products: 84.2 us -> 78 us  [per_device(): jnp.einsum('schw,sohw->co', inputs, delta_pre, preferred_element_type=jnp...]
  transfers between devices with their start and end apart: 4 -> 4, of which waited for: 2 -> 2; matrix products, arithmetic and copies ran while one was open for 30% -> 31% of each run, Pallas kernels for 0% -> 0%
where the time goes in v1:
time: 464 us; the launch traced here: 461 us
  matrix products  271 us (58%)
  blocking collectives  62.9 us (14%)
  waiting for transfers between devices  60.6 us (13%)
  local copies, waits for them, and re-layouts  23.7 us (5%)
  other arithmetic  18.3 us (4%)
  between operations  14.8 us (3%)
  starting transfers between devices  8.74 us (2%)
    dot_general x2, matrix products, row_synth(): jnp.einsum('kpsch,pkw->schw', spectra, basis, preferred_element_type=jnp....  79 us
    dot_general x1, matrix products, per_device(): jnp.einsum('schw,sohw->co', inputs, delta_pre, preferred_element_type=jnp...  78 us
    psum x1, blocking collectives, per_device(): weight_total, bias_total = lax.psum((weight_term, bias_sum), 'space')  62.9 us
    reduce_scatter x2, waiting for transfers between devices, to_modes(): lax.psum_scatter(column_modes(row_modes, own_basis), 'space', scatter_dim...  60.3 us
    dot_general x1, matrix products, per_device(): jnp.einsum('co,sohw->schw', local_weight, delta_pre, preferred_element_ty...  35.8 us
    dot_general x1, matrix products, per_device(): jnp.einsum('co,schw->sohw', local_weight, inputs, preferred_element_type=...  22.5 us
    dot_general x2, matrix products, row_analysis(): jnp.einsum('schw,pkw->kpsch', field_data, basis, preferred_element_type=j...  21.8 us
    unnamed x41, local copies, waits for them, and re-layouts  21 us
  transfers between devices with their start and end apart: 4, of which 2 were waited for; matrix products, arithmetic and copies ran while one was open for 31% of the time, Pallas kernels for 0%

profile of v1, /device:TPU:0, one launch (start us, length us, event | category | flops | bytes accessed | tf_op | source)
XLA Modules:
  0.0 460.6 jit_solution(14848506588378217110)
XLA Ops:
  7.2 2.2 multiply_convert_fusion
  9.8 10.8 %fusion.37 = f32[64,2,32,128]{3,0,2,1:T(8,128)} fusion(bf16[1,32,128,2048]{3,2,1,0:T(8,128)(2,1)} %param.5, bf16[1,64,2048]{2,1,0:T(8,128)(2,1)S(1)} %get-tuple-element.42, bf16[1,64,2048]{2,1,0:T(8,128)(2,1)S(1)} %get-tuple-element.43), kind=kOutput, calls=%fused_computation.52 | convolution fusion | flops 2148532224 | bytes 19398656 | tf_op jit(solution)/shard_map/schw,pkw->kpsch/dot_general | solution.py:47
  20.6 4.9 %fusion.31 = f32[64,2,1,32,128]{4,3,1,0,2:T(8,128)S(1)} fusion(f32[64,2,32,128]{3,0,2,1:T(8,128)} %fusion.37, f32[128,64]{1,0:T(8,128)S(1)} %get-tuple-element.39, f32[128,64]{1,0:T(8,128)S(1)} %get-tuple-element.38), kind=kOutput, calls=%fused_computation.50 | convolution fusion | flops 805322752 | bytes 4259840 | tf_op jit(solution)/shard_map/kpsch,hj->kpscj/dot_general | solution.py:55
  26.2 1.3 pad_maximum_fusion.3
  27.5 60.3 %reduce-scatter.3.cloned.1.call-done = f32[4,1,32,128]{3,2,0,1:T(8,128)} async-done(((f32[64,1,32,128]{3,2,0,1:T(8,128)}), f32[4,1,32,128]{3,2,0,1:T(8,128)}) %reduce-scatter.3.cloned.1.call-update) | async-done | bytes 65552 | tf_op jit(solution)/shard_map/reduce_scatter | solution.py:136
  87.8 1.0 slice_bitcast_fusion.37
  88.8 1.0 multiply_reduce_fusion.6
  90.0 2.9 fusion.66
  92.9 2.9 fusion.73
  95.8 3.5 fusion.25
  99.3 3.2 fusion.26
  102.6 0.6 constant_dynamic-update-slice_fusion.15
  103.3 0.6 constant_dynamic-update-slice_fusion.14
  103.9 0.6 constant_dynamic-update-slice_fusion.13
  104.6 0.6 constant_dynamic-update-slice_fusion.12
  105.2 0.6 constant_dynamic-update-slice_fusion.11
  105.9 0.6 constant_dynamic-update-slice_fusion.10
  106.5 0.6 constant_dynamic-update-slice_fusion.9
  107.2 0.6 constant_dynamic-update-slice_fusion.8
  107.8 0.6 constant_dynamic-update-slice_fusion.7
  108.5 0.6 constant_dynamic-update-slice_fusion.6
  109.1 0.6 constant_dynamic-update-slice_fusion.5
  109.8 0.6 constant_dynamic-update-slice_fusion.4
  110.4 0.6 constant_dynamic-update-slice_fusion.3
  111.1 0.6 constant_dynamic-update-slice_fusion.2
  111.7 0.6 constant_dynamic-update-slice_fusion.1
  112.3 0.6 constant_dynamic-update-slice_fusion
  113.0 4.3 all-to-all-start
  117.4 22.5 %fusion.17 = f32[128,2048,32]{1,2,0:T(8,128)} fusion(bf16[32,128,2048]{2,1,0:T(8,128)(2,1)} %bitcast.372, bf16[32,32]{1,0:T(8,128)(2,1)S(1)} %copy-done), kind=kOutput, calls=%fused_computation.21 | convolution fusion | flops 536870912 | bytes 50333696 | tf_op jit(solution)/shard_map/co,schw->sohw/dot_general | solution.py:146
  140.3 1.3 copy.70
  141.6 45.4 %convert_reduce_fusion = (f32[32]{0:T(128)S(1)}, bf16[1,32,128,2048]{3,2,1,0:T(8,128)(2,1)}) fusion(bf16[1,32,128,2048]{3,2,1,0:T(8,128)(2,1)} %param.6, f32[32]{0:T(128)S(1)} %copy-done.3, f32[128,2048,32]{1,2,0:T(8,128)} %fusion.17, bf16[1,64,2048]{2,1,0:T(8,128)(2,1)S(1)} %get-tuple-element.42, bf16[1,64,2048]{2,1,0:T(8,128)(2,1)S(1)} %get-tuple-element.43, ...), kind=kOutput, calls=%fused_computation.11 | convolution fusion | flops 2290352128 | bytes 68681984 | tf_op jit(solution)/shard_map/kpsch,pkw->schw/dot_general | solution.py:51
  187.0 11.0 %fusion.40 = f32[64,2,32,128]{3,0,2,1:T(8,128)} fusion(bf16[1,32,128,2048]{3,2,1,0:T(8,128)(2,1)} %get-tuple-element.41, bf16[1,64,2048]{2,1,0:T(8,128)(2,1)S(1)} %get-tuple-element.42, bf16[1,64,2048]{2,1,0:T(8,128)(2,1)S(1)} %get-tuple-element.43), kind=kOutput, calls=%fused_computation.53 | convolution fusion | flops 2148532224 | bytes 19398656 | tf_op jit(solution)/shard_map/schw,pkw->kpsch/dot_general | solution.py:47
  198.0 4.6 fusion.34
  203.2 1.3 pad_maximum_fusion.4
  204.5 78.0 %fusion.43 = f32[32,32]{0,1:T(8,128)S(1)} fusion(bf16[32,128,2048]{2,1,0:T(8,128)(2,1)} %bitcast.373, bf16[32,128,2048]{2,1,0:T(8,128)(2,1)} %bitcast.374), kind=kOutput, calls=%fused_computation.60 | convolution fusion | flops 536870912 | bytes 33558528 | tf_op jit(solution)/shard_map/schw,sohw->co/dot_general | solution.py:159
  282.6 62.9 %all-reduce = (f32[32,32]{0,1:T(8,128)S(1)}, f32[32]{0:T(128)S(1)}) all-reduce(f32[32,32]{0,1:T(8,128)S(1)} %fusion.43, f32[32]{0:T(128)S(1)} %get-tuple-element.40), channel_id=1, replica_groups=mesh['dom'=2,'space'=16] {'space'}, use_global_device_ids=true, to_apply=%region_2.3 | all-reduce | flops 1056 | bytes 8448 | tf_op jit(solution)/shard_map/psum | solution.py:161
  345.4 0.9 broadcast_multiply_fusion
  346.4 4.3 add_bitcast_fusion
  350.7 2.9 fusion.63
  353.7 2.9 fusion.70
  356.6 3.2 fusion.23
  359.8 3.2 fusion.24
  363.1 0.6 constant_dynamic-update-slice_fusion.31
  363.8 0.6 constant_dynamic-update-slice_fusion.30
  364.4 0.6 constant_dynamic-update-slice_fusion.29
  365.0 0.6 constant_dynamic-update-slice_fusion.28
  365.7 0.6 constant_dynamic-update-slice_fusion.27
  366.3 0.6 constant_dynamic-update-slice_fusion.26
  366.9 0.6 constant_dynamic-update-slice_fusion.25
  367.6 0.6 constant_dynamic-update-slice_fusion.24
  368.2 0.6 constant_dynamic-update-slice_fusion.23
  368.8 0.6 constant_dynamic-update-slice_fusion.22
  369.5 0.6 constant_dynamic-update-slice_fusion.21
  370.1 0.6 constant_dynamic-update-slice_fusion.20
  370.8 0.6 constant_dynamic-update-slice_fusion.19
  371.4 0.6 constant_dynamic-update-slice_fusion.18
  372.0 0.6 constant_dynamic-update-slice_fusion.17
  372.7 0.7 constant_dynamic-update-slice_fusion.16
  373.3 4.3 all-to-all-start.1
  377.7 0.7 copy.98
  378.9 35.8 %fusion.14 = f32[128,2048,32]{1,2,0:T(8,128)} fusion(bf16[32,128,2048]{2,1,0:T(8,128)(2,1)} %bitcast.375, bf16[32,32]{1,0:T(8,128)(2,1)S(1)} %copy-done), kind=kOutput, calls=%fused_computation.18 | convolution fusion | flops 536870912 | bytes 50333696 | tf_op jit(solution)/shard_map/co,sohw->schw/dot_general | solution.py:155
  414.7 3.6 pad_maximum_fusion
  418.3 1.3 copy.92
  419.6 33.6 %fusion.6 = bf16[1,32,128,2048]{3,2,1,0:T(8,128)(2,1)} fusion(f32[128,2048,32]{1,2,0:T(8,128)} %fusion.14, bf16[64,2,32,128]{3,2,1,0:T(8,128)(2,1)S(1)} %bitcast.376, bf16[1,64,2048]{2,1,0:T(8,128)(2,1)S(1)} %get-tuple-element.42, bf16[1,64,2048]{2,1,0:T(8,128)(2,1)S(1)} %get-tuple-element.43), kind=kOutput, calls=%fused_computation.8 | convolution fusion | flops 2164523008 | bytes 51904512 | tf_op jit(solution)/shard_map/kpsch,pkw->schw/dot_general | solution.py:51
  (30 shorter events, 3.0 us)
Async XLA Ops:
  7.2 110.2 %copy-start = (bf16[32,32]{1,0:T(8,128)(2,1)S(1)}, bf16[32,32]{1,0:T(8,128)(2,1)}, u32[]{:S(2)}) copy-start(bf16[32,32]{1,0:T(8,128)(2,1)} %param.8) | copy-start | bytes 6148
  7.2 80.6 %reduce-scatter.3.cloned.1.call-start = ((), (), s32[]{:S(2)}) async-start(), calls=%async_computation.4 | async-start | bytes 1114112 | tf_op jit(solution)/shard_map/reduce_scatter | solution.py:136
  9.8 79.0 %copy-start.1 = (f32[4,32,32,128]{3,2,1,0:T(8,128)S(1)}, f32[4,32,32,128]{3,2,1,0:T(8,128)}, u32[]{:S(2)}) copy-start(f32[4,32,32,128]{3,2,1,0:T(8,128)} %param.7) | copy-start | bytes 6291460
  113.0 27.3 %all-to-all-start = ((bf16[16,4,2,1,32,128]{5,4,1,2,3,0:T(8,128)(2,1)}), bf16[16,4,2,1,32,128]{5,4,1,2,3,0:T(8,128)(2,1)}, u32[]{:S(2)}, u32[]{:S(2)}) async-start(bf16[16,4,2,1,32,128]{5,4,1,2,3,0:T(8,128)(2,1)} %constant_dynamic-update-slice_fusion), calls=%async_computation.1 | async-start | bytes 2097152 | tf_op jit(solution)/shard_map/all_to_all | solution.py:16
  117.3 228.1 %reduce-scatter.5.cloned.1.call-start = ((), (), s32[]{:S(2)}) async-start(), calls=%async_computation.5 | async-start | bytes 1114112 | tf_op jit(solution)/shard_map/reduce_scatter | solution.py:136
  117.4 24.2 %copy-start.3 = (f32[32]{0:T(128)S(1)}, f32[32]{0:T(128)}, u32[]{:S(2)}) copy-start(f32[32]{0:T(128)} %param.9) | copy-start | bytes 388
  373.3 45.0 %all-to-all-start.1 = ((bf16[16,4,2,1,32,128]{5,4,1,2,3,0:T(8,128)(2,1)}), bf16[16,4,2,1,32,128]{5,4,1,2,3,0:T(8,128)(2,1)}, u32[]{:S(2)}, u32[]{:S(2)}) async-start(bf16[16,4,2,1,32,128]{5,4,1,2,3,0:T(8,128)(2,1)} %constant_dynamic-update-slice_fusion.16), calls=%async_computation.3 | async-start | bytes 2097152 | tf_op jit(solution)/shard_map/all_to_all | solution.py:16
  378.9 35.8 %copy-start.2 = (f32[4,32,32,64]{3,2,1,0:T(8,128)S(1)}, f32[4,32,32,64]{3,2,1,0:T(8,128)}, u32[]{:S(2)}) copy-start(f32[4,32,32,64]{3,2,1,0:T(8,128)} %get-tuple-element.28) | copy-start | bytes 3145732
Sparse Core Ops, SparseCore 0:
  27.6 60.1 reduce-scatter.2
  204.7 59.4 reduce-scatter.4
